TPU v7x, 32 devices: a whole 2x2x4 slice. The times are simulated.
32 devices in a mesh: win: 2 (over y), tile: 4 (over x, core), chan: 4 (over z).
Axes of the slice: x: 2, y: 2, z: 4, core: 2. Of those that a mesh axis runs over, the one named last changes fastest.
Arguments:
- residual: float32 [32, 128, 2048], P(('win', 'tile', 'chan')), parts along dimension 0, may hold values from -6 to 6
- freq_index: int32 [32], P('win'), parts along dimension 0, may hold values from 0 to 1023, as said below
- psf_profile: float32 [32, 2, 257], P(('win', 'tile', 'chan')), parts along dimension 0, may hold values from -0.3 to 0.3
Outputs:
- taylor_step: float32 [3, 256, 2048], P(None, ('win', 'tile'), 'chan'), parts along dimension 1
- new_residual: float32 [32, 128, 2048], P(('win', 'tile', 'chan')), parts along dimension 0
There are 2 independent parts, one for each index of `win`. A program takes and returns all parts, laid end to end along the dimension named above; each array names one. Nothing has to cross between parts.
Inputs may be any that keep to these rules, and one draw needn't show every extreme that they name: `freq_index`: the values are distinct, and both ends of the grid, 0 and 1023, occur.
All inputs are finite; a program needn't handle non-finite values.
Results may differ from a plain program's by a relative error of at most 0.00013.
Values sent between devices are 32-bit elements; how exact they have to be, the bound alone decides.
A program may use at most 64 MiB of HBM per device.

v0:
```python
import jax
import jax.numpy as jnp
from jax import lax
from jax.sharding import PartitionSpec as P

FREQS = 1024


highest = lax.Precision.HIGHEST


def spectral_weights(freq_index):
    offset = 2.0 * freq_index.astype(jnp.float32) / (FREQS - 1) - 1.0
    return jnp.stack([jnp.ones_like(offset), offset, offset * offset])


def inverse_three(matrix):
    first_row, second_row, third_row = (matrix[0], matrix[1], matrix[2])
    cross_one = jnp.cross(second_row, third_row)
    cross_two = jnp.cross(third_row, first_row)
    cross_three = jnp.cross(first_row, second_row)
    determinant = jnp.sum(first_row * cross_one)
    return jnp.stack([cross_one, cross_two, cross_three], axis=1) / determinant


def band_blocks(profile):
    half_width = (profile.shape[0] - 1) // 2
    extended = jnp.pad(profile, (383 - half_width, 383 - half_width))
    blocks = []
    for shift in (-1, 0, 1):
        window = extended[128 * shift + 256 : 128 * shift + 511][::-1]
        padded = jnp.concatenate([window, jnp.zeros((1,), window.dtype)])
        tiled = jnp.tile(padded, 128)
        skewed = tiled[127 : 127 + 128 * 255].reshape(128, 255)[:, :128]
        blocks.append(skewed)
    return jnp.stack(blocks)


def along_last(field, blocks):
    count = field.shape[-1] // 128
    shaped = field.reshape(field.shape[:-1] + (count, 128))
    padded = jnp.pad(shaped, [(0, 0)] * (field.ndim - 1) + [(1, 1), (0, 0)])
    result = jnp.einsum("...bi,io->...bo", padded[..., 0:count, :], blocks[0], precision=highest)
    result = result + jnp.einsum(
        "...bi,io->...bo", padded[..., 1 : count + 1, :], blocks[1], precision=highest
    )
    result = result + jnp.einsum(
        "...bi,io->...bo", padded[..., 2 : count + 2, :], blocks[2], precision=highest
    )
    return result.reshape(field.shape)


def along_first(field, blocks):
    count = field.shape[0] // 128
    shaped = field.reshape((count, 128, field.shape[1]))
    padded = jnp.pad(shaped, [(1, 1), (0, 0), (0, 0)])
    result = jnp.einsum("biw,io->bow", padded[0:count], blocks[0], precision=highest)
    result = result + jnp.einsum("biw,io->bow", padded[1 : count + 1], blocks[1], precision=highest)
    result = result + jnp.einsum("biw,io->bow", padded[2 : count + 2], blocks[2], precision=highest)
    return result.reshape(field.shape)


def shards(residual, freq_index, psf_profile):
    weights = spectral_weights(freq_index)
    hessian = jnp.dot(weights, weights.T, precision=highest)
    solver = inverse_three(hessian)
    channels = residual.shape[0]
    height = residual.shape[1]
    width = residual.shape[2]
    first_channel = lax.axis_index(("tile", "chan")) * channels
    local_weights = lax.dynamic_slice_in_dim(weights, first_channel, channels, 1)
    row_tiles = lax.axis_size("tile")
    col_tiles = lax.axis_size("chan")
    block_rows = height // row_tiles
    block_cols = width // col_tiles
    along_rows = jax.vmap(band_blocks)(psf_profile[:, 1])
    along_cols = jax.vmap(band_blocks)(psf_profile[:, 0])
    split = residual.reshape(channels, row_tiles, block_rows, col_tiles, block_cols)
    terms = jnp.einsum("tc,cahbw->abthw", local_weights, split, precision=highest)
    terms = terms.reshape(row_tiles * col_tiles * 3, block_rows, block_cols)
    gradient = lax.psum_scatter(terms, ("tile", "chan"), scatter_dimension=0, tiled=True)
    taylor_step = jnp.einsum("ts,shw->thw", solver, gradient, precision=highest)
    pieces = jnp.einsum(
        "tc,ktrw->kcrw",
        local_weights,
        lax.all_gather(taylor_step[None], ("tile", "chan"), axis=0, tiled=True),
        precision=highest,
    )
    model = pieces.reshape(row_tiles, col_tiles, channels, block_rows, block_cols)
    model = model.transpose(2, 0, 3, 1, 4).reshape(channels, height, width)
    rowwise = jax.vmap(along_last)(model, along_rows)
    blurred = jax.vmap(along_first)(rowwise, along_cols)
    return (taylor_step, residual - blurred)


def solution(mesh):
    in_specs = (
        P(("win", "tile", "chan"), None, None),
        P("win"),
        P(("win", "tile", "chan"), None, None),
    )
    out_specs = (P(None, ("win", "tile"), "chan"), P(("win", "tile", "chan"), None, None))
    return jax.shard_map(shards, mesh=mesh, in_specs=in_specs, out_specs=out_specs, check_vma=False)
```

profile of v0, /device:TPU:0, one launch (start us, length us, event | category | flops | bytes accessed | tf_op | source)
XLA Modules:
  0.0 157.5 jit_solution(13836294157048011253)
XLA Ops:
  7.2 0.7 fusion.18
  7.9 1.9 %reshape.150 = f32[4,32,4,512]{3,2,1,0:T(4,128)S(1)} reshape(f32[1,128,2048]{2,1,0:T(8,128)} %param.5) | data formatting | bytes 2097152 | tf_op jit(solution)/shard_map/reshape
  9.8 0.3 copy.25
  10.2 0.2 dynamic-slice_reduce_fusion
  10.4 2.2 %broadcast_multiply_fusion = f32[3,4,32,4,512]{4,2,0,3,1:T(8,128)} fusion(f32[4,32,4,512]{3,1,2,0:T(8,128)S(1)} %copy.25, f32[3]{0:T(128)S(1)} %dynamic-slice_reduce_fusion), kind=kLoop, calls=%fused_computation.6 | loop fusion | flops 786432 | bytes 4194316 | tf_op jit(solution)/shard_map/tc,cahbw->abthw/dot_general | solution.py:79
  12.7 0.2 fusion.24
  12.9 0.7 fusion.25
  21.0 0.7 fusion.27
  37.2 0.7 multiply_reduce_fusion
  38.3 43.4 %reduce-scatter.2.cloned.1.call-done = f32[3,32,512]{2,1,0:T(8,128)} async-done(((f32[48,32,512]{2,1,0:T(8,128)}), f32[3,32,512]{2,1,0:T(8,128)}) %reduce-scatter.2.cloned.1.call-update) | async-done | bytes 196624 | tf_op jit(solution)/shard_map/reduce_scatter | solution.py:81
  81.7 2.2 %fusion.13 = f32[3,32,512]{2,0,1:T(4,128)S(1)} fusion(f32[3,32,512]{2,1,0:T(8,128)} %reduce-scatter.2.cloned.1.call-done, f32[3,1]{1,0:T(4,128)S(1)} %copy.24, f32[3,1]{1,0:T(4,128)S(1)} %copy.23, f32[3,1]{1,0:T(4,128)S(1)} %copy.22, f32[]{:T(128)} %get-tuple-element.9), kind=kOutput, calls=%fused_computation.19 | convolution fusion | flops 1769499 | bytes 393256 | tf_op jit(solution)/shard_map/ts,shw->thw/dot_general | solution.py:82
  84.0 0.7 copy.33
  84.8 0.3 reverse
  85.3 0.2 reverse.5
  85.7 0.1 copy.43
  85.8 0.4 slice_reduce_fusion.2
  86.2 0.3 reshape.159
  86.6 0.2 reverse.3
  86.9 0.2 reverse.4
  87.3 0.1 copy.44
  87.4 0.4 slice_reduce_fusion.1
  87.8 0.3 reshape.160
  88.2 0.1 copy.45
  88.4 0.4 slice_reduce_fusion
  88.8 0.3 reshape.161
  89.2 0.1 copy.42
  89.4 0.4 slice_reduce_fusion.3
  89.7 0.3 reshape.154
  90.1 0.2 reverse.1
  90.4 0.2 reverse.2
  90.7 0.1 copy.41
  90.8 0.4 slice_reduce_fusion.4
  91.2 0.3 reshape.153
  91.6 0.1 copy.40
  91.7 0.4 slice_reduce_fusion.5
  92.1 0.3 reshape.152
  92.5 0.6 fusion.11
  93.2 35.7 %all-gather.3.cloned.1.call-done = f32[48,32,512]{2,1,0:T(8,128)} async-done(((f32[3,32,512]{2,1,0:T(8,128)}), f32[48,32,512]{2,1,0:T(8,128)}) %all-gather.3.cloned.1.call-update) | async-done | bytes 3145744 | tf_op jit(solution)/shard_map/all_gather | solution.py:86
  128.8 11.5 %fusion = f32[1,4,4,32,512]{4,0,3,2,1:T(1,128)S(1)} fusion(f32[4,4,32,512,3]{3,2,4,1,0:T(8,128)} %bitcast.132, f32[3]{0:T(128)S(1)} %dynamic-slice_reduce_fusion), kind=kOutput, calls=%fused_computation | convolution fusion | flops 9437184 | bytes 4194316 | tf_op jit(solution)/shard_map/tc,ktrw->kcrw/dot_general | solution.py:83
  140.3 0.7 copy.53
  141.0 1.4 reshape_reshape.3
  142.4 0.4 reshape.163
  142.8 1.6 copy.28
  144.4 1.1 fusion.5
  145.4 1.4 convolution_add_fusion.3
  146.8 1.1 convolution_add_fusion.2
  147.9 1.1 convolution_add_fusion.1
  149.0 1.7 %fusion.3 = f32[1,128,2048]{2,1,0:T(8,128)} fusion(f32[1,128,2048]{2,1,0:T(8,128)S(1)} %copy-done, f32[128,2048]{1,0:T(8,128)S(1)} %convolution_add_fusion.1, f32[1,3,128,128]{3,2,1,0:T(8,128)S(1)} %maximum_bitcast_fusion), kind=kOutput, calls=%fused_computation.5 | convolution fusion | flops 403177472 | bytes 3211264 | tf_op jit(solution)/shard_map/vmap(biw,io->bow)/dot_general | solution.py:59
  (45 shorter events, 1.9 us)
Async XLA Ops:
  7.2 74.6 %reduce-scatter.2.cloned.1.call-start = ((), (), s32[]{:S(2)}) async-start(), calls=%async_computation.1 | async-start | bytes 3342336 | tf_op jit(solution)/shard_map/reduce_scatter | solution.py:81
  12.6 72.2 %copy-start.1 = (f32[1,2,257]{2,1,0:T(2,128)S(1)}, f32[1,2,257]{2,1,0:T(2,128)}, u32[]{:S(2)}) copy-start(f32[1,2,257]{2,1,0:T(2,128)} %param.7) | copy-start | bytes 6172
  12.6 116.2 %all-gather.3.cloned.1.call-start = ((), (), s32[]{:S(2)}) async-start(), calls=%async_computation.2 | async-start | bytes 3342336 | tf_op jit(solution)/shard_map/all_gather | solution.py:86
  146.8 2.2 %copy-start = (f32[1,128,2048]{2,1,0:T(8,128)S(1)}, f32[1,128,2048]{2,1,0:T(8,128)}, u32[]{:S(2)}) copy-start(f32[1,128,2048]{2,1,0:T(8,128)} %param.5) | copy-start | bytes 3145732
Sparse Core Ops, SparseCore 0:
  12.7 68.9 reduce-scatter.1
  84.9 43.9 all-gather.2
where the time goes:
time: 158 us
  waiting for transfers between devices  79.1 us (50%)
  between operations  37.4 us (24%)
  matrix products  20.8 us (13%)
  local copies, waits for them, and re-layouts  16.2 us (10%)
  other arithmetic  3.99 us (3%)
    reduce_scatter x1, waiting for transfers between devices, shards(): lax.psum_scatter(terms, ('tile', 'chan'), scatter_dimension=0, tiled=True)  43.4 us
    all_gather x1, waiting for transfers between devices, shards(): lax.all_gather(taylor_step[None], ('tile', 'chan'), axis=0, tiled=True)  35.7 us
    dot_general x1, matrix products, shards(): jnp.einsum('tc,ktrw->kcrw', local_weights, lax.all_gather(taylor_step[Non...  11.5 us
    unnamed x32, local copies, waits for them, and re-layouts  3.62 us
  transfers between devices with their start and end apart: 2, of which 2 were waited for; matrix products, arithmetic and copies ran while one was open for 7% of the time, Pallas kernels for 0%

commit v1 on v0

v1 whole, which is shorter than its diff:
```python
import functools

import jax
import jax.numpy as jnp
from jax import lax
from jax.experimental import pallas as pl
from jax.experimental.pallas import tpu as pltpu
from jax.sharding import PartitionSpec as P

FREQS = 1024
MESH = pl.DeviceIdType.MESH
HOP = 2
CHUNK = 256


def split_halves(x):
    high = x.astype(jnp.bfloat16)
    low = (x - high.astype(jnp.float32)).astype(jnp.bfloat16)
    return high, low


def dot_split(a, b, dims):
    def one(x, y):
        return lax.dot_general(x, y, (dims, ((), ())), preferred_element_type=jnp.float32)

    return one(a[0], b[0]) + (one(a[0], b[1]) + one(a[1], b[0]))


def kernel(
    tiles, depth, chunks, res, freq, psf, taylor_out, new_out,
    raw, part, left_in, right_in, left_sum, right_sum, steps, outgoing, model,
    profile, row_high, row_low, col_high, col_low, weight_s,
    raw_send, raw_recv, mod_send, mod_recv, rt_send, rt_recv, lf_send, lf_recv,
):
    a = lax.axis_index("tile")
    k = lax.axis_index("chan")
    height = res.shape[1]
    rows = height // tiles
    total = freq.shape[0]

    def member(d):
        return lax.rem(a + d, tiles)

    barrier = pltpu.get_barrier_semaphore()
    for d in range(1, tiles):
        pl.semaphore_signal(barrier, inc=1, device_id={"tile": member(d)}, device_id_type=MESH)

    @pl.when(k > 0)
    def _():
        pl.semaphore_signal(barrier, inc=1, device_id={"chan": k - 1}, device_id_type=MESH)

    @pl.when(k < depth - 1)
    def _():
        pl.semaphore_signal(barrier, inc=1, device_id={"chan": k + 1}, device_id_type=MESH)

    ends = jnp.where(k > 0, 1, 0) + jnp.where(k < depth - 1, 1, 0)
    pl.semaphore_wait(barrier, tiles - 1 + ends)

    def own_rows(b):
        return pl.ds(pl.multiple_of(b * rows, rows), rows)

    def columns(j):
        return pl.ds(pl.multiple_of(j * CHUNK, CHUNK), CHUNK)

    def raw_copy(j, d):
        return pltpu.make_async_remote_copy(
            src_ref=res.at[0, own_rows(member(d)), columns(j)],
            dst_ref=raw.at[j, d - 1],
            send_sem=raw_send.at[j, d - 1],
            recv_sem=raw_recv.at[j, d - 1],
            device_id={"tile": member(d)},
            device_id_type=MESH,
        )

    def model_copy(j, d):
        return pltpu.make_async_remote_copy(
            src_ref=outgoing.at[j, d - 1],
            dst_ref=model.at[j + 1, own_rows(a)],
            send_sem=mod_send.at[j, d - 1],
            recv_sem=mod_recv.at[j, d - 1],
            device_id={"tile": member(d)},
            device_id_type=MESH,
        )

    def right_copy(j):
        return pltpu.make_async_remote_copy(
            src_ref=left_sum.at[j], dst_ref=left_in.at[j],
            send_sem=rt_send.at[j], recv_sem=rt_recv.at[j],
            device_id={"chan": lax.rem(k + 1, depth)}, device_id_type=MESH,
        )

    def left_copy(j):
        return pltpu.make_async_remote_copy(
            src_ref=right_sum.at[j], dst_ref=right_in.at[j],
            send_sem=lf_send.at[j], recv_sem=lf_recv.at[j],
            device_id={"chan": lax.rem(k + depth - 1, depth)}, device_id_type=MESH,
        )

    def send_raw(j, carry):
        for d in range(1, tiles):
            raw_copy(j, d).start()
        return carry

    lax.fori_loop(0, chunks, send_raw, 0)

    def offset_of(c):
        return 2.0 * freq[c].astype(jnp.float32) / (FREQS - 1) - 1.0

    def add_powers(c, sums):
        x = offset_of(c)
        y = x * x
        return sums[0] + x, sums[1] + y, sums[2] + x * y, sums[3] + y * y

    zero = jnp.float32(0.0)
    s1, s2, s3, s4 = lax.fori_loop(0, total, add_powers, (zero, zero, zero, zero))
    m = ((jnp.float32(total), s1, s2), (s1, s2, s3), (s2, s3, s4))

    def cross(p, q):
        return (p[1] * q[2] - p[2] * q[1], p[2] * q[0] - p[0] * q[2], p[0] * q[1] - p[1] * q[0])

    crosses = (cross(m[1], m[2]), cross(m[2], m[0]), cross(m[0], m[1]))
    det = m[0][0] * crosses[0][0] + m[0][1] * crosses[0][1] + m[0][2] * crosses[0][2]
    for t in range(3):
        for s in range(3):
            weight_s[2 * tiles + 3 * t + s] = crosses[s][t] / det
    for d in range(tiles):
        x = offset_of(member(d) * depth + k)
        weight_s[2 * d] = x
        weight_s[2 * d + 1] = x * x

    profile[...] = jnp.zeros_like(profile)
    profile[:, 0 : psf.shape[2]] = psf[0]
    wide = profile.shape[1]
    band = pltpu.roll(
        jnp.broadcast_to(profile[1:2, :], (CHUNK, wide)), 0, 1, stride=1, stride_axis=0
    )
    row_high[...], row_low[...] = split_halves(band)
    half = (psf.shape[2] - 1) // 2
    band = pltpu.roll(
        jnp.broadcast_to(profile[0:1, :], (height, wide)), wide - half, 1, stride=1, stride_axis=0
    )[:, :height]
    col_high[...], col_low[...] = split_halves(band)
    model[0] = jnp.zeros(model.shape[1:], jnp.float32)
    model[chunks + 1] = jnp.zeros(model.shape[1:], jnp.float32)

    lag_left = HOP * k
    lag_right = HOP * (depth - 1 - k)
    lag = jnp.maximum(lag_left, lag_right)

    def inside(j):
        return jnp.logical_and(j >= 0, j < chunks)

    def step(s, carry):
        @pl.when(s < chunks)
        def _():
            j = s
            own = res[0, own_rows(a), columns(j)]
            sums = [own, own * weight_s[0], own * weight_s[1]]
            for d in range(1, tiles):
                raw_copy(j, d).wait_recv()
            for d in range(1, tiles):
                e = tiles - d
                piece = raw[j, d - 1]
                sums[0] += piece
                sums[1] += piece * weight_s[2 * e]
                sums[2] += piece * weight_s[2 * e + 1]
            for t in range(3):
                part[j, t] = sums[t]

        jl = s - lag_left

        @pl.when(inside(jl))
        def _():
            @pl.when(k == 0)
            def _():
                left_sum[jl] = part[jl]

            @pl.when(k > 0)
            def _():
                right_copy(jl).wait_recv()
                left_sum[jl] = left_in[jl] + part[jl]

            @pl.when(k < depth - 1)
            def _():
                right_copy(jl).start()

        jr = s - lag_right

        @pl.when(inside(jr))
        def _():
            @pl.when(k == depth - 1)
            def _():
                right_sum[jr] = part[jr]

            @pl.when(k < depth - 1)
            def _():
                left_copy(jr).wait_recv()
                right_sum[jr] = right_in[jr] + part[jr]

            @pl.when(k > 0)
            def _():
                left_copy(jr).start()

        jt = s - lag

        @pl.when(inside(jt))
        def _():
            @pl.when(k == 0)
            def _():
                steps[jt] = right_sum[jt]

            @pl.when(k > 0)
            def _():
                steps[jt] = left_in[jt] + right_sum[jt]

            g = [steps[jt, t] for t in range(3)]
            base = 2 * tiles
            u = [
                weight_s[base + 3 * t] * g[0]
                + weight_s[base + 3 * t + 1] * g[1]
                + weight_s[base + 3 * t + 2] * g[2]
                for t in range(3)
            ]
            for t in range(3):
                steps[jt, t] = u[t]
            for d in range(1, tiles):
                outgoing[jt, d - 1] = u[0] + weight_s[2 * d] * u[1] + weight_s[2 * d + 1] * u[2]
                model_copy(jt, d).start()
            model[jt + 1, own_rows(a)] = u[0] + weight_s[0] * u[1] + weight_s[1] * u[2]

        jb = jt - 1

        @pl.when(jnp.logical_and(jb + 1 >= 0, jb + 1 < chunks))
        def _():
            for d in range(1, tiles):
                model_copy(jb + 1, d).wait_recv()

        @pl.when(inside(jb))
        def _():
            field = jnp.concatenate(
                [model[jb, :, CHUNK - half :], model[jb + 1], model[jb + 2, :, :half]], axis=1
            )
            rowwise = dot_split(split_halves(field), (row_high[...], row_low[...]), ((1,), (1,)))
            blurred = dot_split((col_high[...], col_low[...]), split_halves(rowwise), ((1,), (0,)))
            new_out[0, :, columns(jb)] = res[0, :, columns(jb)] - blurred

        return carry

    lax.fori_loop(0, chunks + HOP * (depth - 1) + 1, step, 0)

    per = taylor_out.shape[2] // CHUNK
    for i in range(per):
        taylor_out[:, :, i * CHUNK : (i + 1) * CHUNK] = steps[k * per + i]

    def drain(j, carry):
        for d in range(1, tiles):
            raw_copy(j, d).wait_send()
            model_copy(j, d).wait_send()

        @pl.when(k < depth - 1)
        def _():
            right_copy(j).wait_send()

        @pl.when(k > 0)
        def _():
            left_copy(j).wait_send()

        return carry

    lax.fori_loop(0, chunks, drain, 0)


def solution(mesh):
    tiles, depth = mesh.shape["tile"], mesh.shape["chan"]

    def shards(residual, freq_index, psf_profile):
        _, height, width = residual.shape
        rows, block = height // tiles, width // depth
        chunks = width // CHUNK
        half = (psf_profile.shape[2] - 1) // 2
        f32, bf16 = jnp.float32, jnp.bfloat16
        chain = pltpu.VMEM((chunks, 3, rows, CHUNK), f32)
        vmem = pl.BlockSpec(memory_space=pltpu.VMEM)
        dma = pltpu.SemaphoreType.DMA
        return pl.pallas_call(
            functools.partial(kernel, tiles, depth, chunks),
            out_shape=(
                jax.ShapeDtypeStruct((3, rows, block), f32),
                jax.ShapeDtypeStruct(residual.shape, f32),
            ),
            in_specs=[vmem, pl.BlockSpec(memory_space=pltpu.SMEM), vmem],
            out_specs=(vmem, vmem),
            scratch_shapes=[
                pltpu.VMEM((chunks, tiles - 1, rows, CHUNK), f32),
                chain, chain, chain, chain, chain, chain,
                pltpu.VMEM((chunks, tiles - 1, rows, CHUNK), f32),
                pltpu.VMEM((chunks + 2, height, CHUNK), f32),
                pltpu.VMEM((2, CHUNK + 2 * half), f32),
                pltpu.VMEM((CHUNK, CHUNK + 2 * half), bf16),
                pltpu.VMEM((CHUNK, CHUNK + 2 * half), bf16),
                pltpu.VMEM((height, height), bf16),
                pltpu.VMEM((height, height), bf16),
                pltpu.SMEM((2 * tiles + 9,), f32),
                dma((chunks, tiles - 1)), dma((chunks, tiles - 1)),
                dma((chunks, tiles - 1)), dma((chunks, tiles - 1)),
                dma((chunks,)), dma((chunks,)), dma((chunks,)), dma((chunks,)),
            ],
            compiler_params=pltpu.CompilerParams(
                collective_id=0, has_side_effects=True, vmem_limit_bytes=40 * 1024 * 1024
            ),
        )(residual, freq_index, psf_profile)

    in_specs = (
        P(("win", "tile", "chan"), None, None),
        P("win"),
        P(("win", "tile", "chan"), None, None),
    )
    out_specs = (P(None, ("win", "tile"), "chan"), P(("win", "tile", "chan"), None, None))
    return jax.shard_map(shards, mesh=mesh, in_specs=in_specs, out_specs=out_specs, check_vma=False)
```

time: 158 us -> 59.4 us (0.38)
  waiting for transfers between devices: 79.1 us -> 0 us
  Pallas kernels: 0 us -> 54.4 us
  between operations: 37.4 us -> 0.65 us
  matrix products: 20.8 us -> 0 us
  local copies, waits for them, and re-layouts: 16.2 us -> 4.21 us
  other arithmetic: 3.99 us -> 0 us
    pallas_call x0 -> x1, Pallas kernels: none -> 54.4 us  [shards(): pl.pallas_call(functools.partial(kernel, tiles, depth, chunks), out_shape...]
    reduce_scatter x1 -> x0, waiting for transfers between devices: 43.4 us -> none  [shards(): lax.psum_scatter(terms, ('tile', 'chan'), scatter_dimension=0, tiled=True)]
    all_gather x1 -> x0, waiting for transfers between devices: 35.7 us -> none  [shards(): lax.all_gather(taylor_step[None], ('tile', 'chan'), axis=0, tiled=True)]
    dot_general x9 -> x0, matrix products: 20.8 us -> none  [the longest x1 11.5 us: shards(): jnp.einsum('tc,ktrw->kcrw', local_weights, lax.all_gather(taylor_step[Non...]
    reshape x8 -> x0, local copies, waits for them, and re-layouts: 4.26 us -> none
    slice x13 -> x0, local copies, waits for them, and re-layouts: 3.71 us -> none  [the longest x9 2.21 us: band_blocks(): skewed = tiled[127:127 + 128 * 255].reshape(128, 255)[:, :128]]
    another operation x10 -> x0, local copies, waits for them, and re-layouts: 3.68 us -> none  [the longest x2 2.96 us: along_last(): shaped = field.reshape(field.shape[:-1] + (count, 128))]
    dot_general x1 -> x0, other arithmetic: 2.16 us -> none  [shards(): jnp.einsum('tc,cahbw->abthw', local_weights, split, precision=highest)]
  transfers between devices with their start and end apart: 2 -> 0, of which waited for: 2 -> 0; matrix products, arithmetic and copies ran while one was open for 7% -> 0% of each run, Pallas kernels for 0% -> 0%
where the time goes in v1:
time: 59.4 us; the launch traced here: 59.2 us
  Pallas kernels  54.4 us (92%)
  local copies, waits for them, and re-layouts  4.21 us (7%)
  between operations  0.65 us (1%)
    pallas_call x1, Pallas kernels, shards(): pl.pallas_call(functools.partial(kernel, tiles, depth, chunks), out_shape...  54.4 us
    unnamed x8, local copies, waits for them, and re-layouts  4.21 us

profile of v1, /device:TPU:0, one launch (start us, length us, event | category | flops | bytes accessed | tf_op | source)
XLA Modules:
  0.0 59.2 jit_solution(15127085458933405483)
XLA Ops:
  0.6 0.0 copy-start
  0.6 1.2 %copy-done = f32[1,128,2048]{2,1,0:T(8,128)S(1)} copy-done((f32[1,128,2048]{2,1,0:T(8,128)S(1)}, f32[1,128,2048]{2,1,0:T(8,128)}, u32[]{:S(2)}) %copy-start) | copy-done | bytes 1048600
  1.9 0.0 copy-start.1
  1.9 0.7 %copy-done.1 = f32[1,2,257]{2,1,0:T(2,128)S(1)} copy-done((f32[1,2,257]{2,1,0:T(2,128)S(1)}, f32[1,2,257]{2,1,0:T(2,128)}, u32[]{:S(2)}) %copy-start.1) | copy-done | bytes 2080
  2.5 0.0 copy-start.2
  2.5 0.7 %copy-done.2 = s32[16]{0:T(128)S(1)} copy-done((s32[16]{0:T(128)S(1)}, s32[16]{0:T(128)}, u32[]{:S(2)}) %copy-start.2) | copy-done | bytes 88
  3.2 54.4 %shard_map.50 = (f32[3,32,512]{2,1,0:T(8,128)S(1)}, f32[1,128,2048]{2,1,0:T(8,128)S(1)}) custom-call(f32[1,128,2048]{2,1,0:T(8,128)S(1)} %copy-done, s32[16]{0:T(128)S(1)} %copy-done.2, f32[1,2,257]{2,1,0:T(2,128)S(1)} %copy-done.1), custom_call_target="tpu_custom_call" | custom-call | tf_op jit(solution)/shard_map/pallas_call | solution.py:285
  57.6 0.7 %copy.7 = f32[3,32,512]{2,1,0:T(8,128)} copy(f32[3,32,512]{2,1,0:T(8,128)S(1)} %get-tuple-element.4) | data formatting | bytes 393216
  58.3 1.0 %copy.8 = f32[1,128,2048]{2,1,0:T(8,128)} copy(f32[1,128,2048]{2,1,0:T(8,128)S(1)} %get-tuple-element.5) | data formatting | bytes 2097152
Async XLA Ops:
  0.6 1.2 %copy-start = (f32[1,128,2048]{2,1,0:T(8,128)S(1)}, f32[1,128,2048]{2,1,0:T(8,128)}, u32[]{:S(2)}) copy-start(f32[1,128,2048]{2,1,0:T(8,128)} %res.1) | copy-start | bytes 3145732
  1.9 0.7 %copy-start.1 = (f32[1,2,257]{2,1,0:T(2,128)S(1)}, f32[1,2,257]{2,1,0:T(2,128)}, u32[]{:S(2)}) copy-start(f32[1,2,257]{2,1,0:T(2,128)} %psf.1) | copy-start | bytes 6172
  2.5 0.7 %copy-start.2 = (s32[16]{0:T(128)S(1)}, s32[16]{0:T(128)}, u32[]{:S(2)}) copy-start(s32[16]{0:T(128)} %freq.1) | copy-start | bytes 196

commit v2 on v1

--- a/solution.py
+++ b/solution.py
@@ -10,6 +10,7 @@
 FREQS = 1024
 MESH = pl.DeviceIdType.MESH
 HOP = 2
+BACK = 3
 CHUNK = 256
 
 
@@ -228,7 +229,7 @@
                 model_copy(jt, d).start()
             model[jt + 1, own_rows(a)] = u[0] + weight_s[0] * u[1] + weight_s[1] * u[2]
 
-        jb = jt - 1
+        jb = jt - BACK
 
         @pl.when(jnp.logical_and(jb + 1 >= 0, jb + 1 < chunks))
         def _():
@@ -246,7 +247,7 @@
 
         return carry
 
-    lax.fori_loop(0, chunks + HOP * (depth - 1) + 1, step, 0)
+    lax.fori_loop(0, chunks + HOP * (depth - 1) + BACK, step, 0)
 
     per = taylor_out.shape[2] // CHUNK
     for i in range(per):

time: 59.4 us -> 45.9 us (0.77)
  Pallas kernels: 54.4 us -> 40.9 us
    pallas_call x1, Pallas kernels: 54.4 us -> 40.9 us  [shards(): pl.pallas_call(functools.partial(kernel, tiles, depth, chunks), out_shape...]
where the time goes in v2:
time: 45.9 us; the launch traced here: 45.8 us
  Pallas kernels  40.9 us (89%)
  local copies, waits for them, and re-layouts  4.21 us (9%)
  between operations  0.65 us (1%)
    pallas_call x1, Pallas kernels, shards(): pl.pallas_call(functools.partial(kernel, tiles, depth, chunks), out_shape...  40.9 us
    unnamed x8, local copies, waits for them, and re-layouts  4.21 us

profile of v2, /device:TPU:0, one launch (start us, length us, event | category | flops | bytes accessed | tf_op | source)
XLA Modules:
  0.0 45.8 jit_solution(10232439660768567281)
XLA Ops:
  0.6 0.0 copy-start
  0.6 1.2 %copy-done = f32[1,128,2048]{2,1,0:T(8,128)S(1)} copy-done((f32[1,128,2048]{2,1,0:T(8,128)S(1)}, f32[1,128,2048]{2,1,0:T(8,128)}, u32[]{:S(2)}) %copy-start) | copy-done | bytes 1048600
  1.9 0.0 copy-start.1
  1.9 0.7 %copy-done.1 = f32[1,2,257]{2,1,0:T(2,128)S(1)} copy-done((f32[1,2,257]{2,1,0:T(2,128)S(1)}, f32[1,2,257]{2,1,0:T(2,128)}, u32[]{:S(2)}) %copy-start.1) | copy-done | bytes 2080
  2.5 0.0 copy-start.2
  2.5 0.7 %copy-done.2 = s32[16]{0:T(128)S(1)} copy-done((s32[16]{0:T(128)S(1)}, s32[16]{0:T(128)}, u32[]{:S(2)}) %copy-start.2) | copy-done | bytes 88
  3.2 40.9 %shard_map.50 = (f32[3,32,512]{2,1,0:T(8,128)S(1)}, f32[1,128,2048]{2,1,0:T(8,128)S(1)}) custom-call(f32[1,128,2048]{2,1,0:T(8,128)S(1)} %copy-done, s32[16]{0:T(128)S(1)} %copy-done.2, f32[1,2,257]{2,1,0:T(2,128)S(1)} %copy-done.1), custom_call_target="tpu_custom_call" | custom-call | tf_op jit(solution)/shard_map/pallas_call | solution.py:286
  44.1 0.7 %copy.7 = f32[3,32,512]{2,1,0:T(8,128)} copy(f32[3,32,512]{2,1,0:T(8,128)S(1)} %get-tuple-element.4) | data formatting | bytes 393216
  44.8 1.0 %copy.8 = f32[1,128,2048]{2,1,0:T(8,128)} copy(f32[1,128,2048]{2,1,0:T(8,128)S(1)} %get-tuple-element.5) | data formatting | bytes 2097152
Async XLA Ops:
  0.6 1.2 %copy-start = (f32[1,128,2048]{2,1,0:T(8,128)S(1)}, f32[1,128,2048]{2,1,0:T(8,128)}, u32[]{:S(2)}) copy-start(f32[1,128,2048]{2,1,0:T(8,128)} %res.1) | copy-start | bytes 3145732
  1.9 0.7 %copy-start.1 = (f32[1,2,257]{2,1,0:T(2,128)S(1)}, f32[1,2,257]{2,1,0:T(2,128)}, u32[]{:S(2)}) copy-start(f32[1,2,257]{2,1,0:T(2,128)} %psf.1) | copy-start | bytes 6172
  2.5 0.7 %copy-start.2 = (s32[16]{0:T(128)S(1)}, s32[16]{0:T(128)}, u32[]{:S(2)}) copy-start(s32[16]{0:T(128)} %freq.1) | copy-start | bytes 196

commit v3 on v2

--- a/solution.py
+++ b/solution.py
@@ -9,9 +9,9 @@
 
 FREQS = 1024
 MESH = pl.DeviceIdType.MESH
-HOP = 2
-BACK = 3
-CHUNK = 256
+HOP = 4
+BACK = 6
+CHUNK = 128
 
 
 def split_halves(x):
@@ -28,10 +28,12 @@
 
 
 def kernel(
-    tiles, depth, chunks, res, freq, psf, taylor_out, new_out,
+    tiles, depth, chunks, res_hbm, freq_hbm, psf_hbm, taylor_out, new_out,
+    res, freq, psf, result,
     raw, part, left_in, right_in, left_sum, right_sum, steps, outgoing, model,
     profile, row_high, row_low, col_high, col_low, weight_s,
     raw_send, raw_recv, mod_send, mod_recv, rt_send, rt_recv, lf_send, lf_recv,
+    local, out_sem, step_sem,
 ):
     a = lax.axis_index("tile")
     k = lax.axis_index("chan")
@@ -39,6 +41,14 @@
     rows = height // tiles
     total = freq.shape[0]
 
+    loads = [
+        pltpu.make_async_copy(freq_hbm, freq, local.at[0]),
+        pltpu.make_async_copy(psf_hbm, psf, local.at[1]),
+        pltpu.make_async_copy(res_hbm, res, local.at[2]),
+    ]
+    for load in loads:
+        load.start()
+
     def member(d):
         return lax.rem(a + d, tiles)
 
@@ -65,7 +75,7 @@
 
     def raw_copy(j, d):
         return pltpu.make_async_remote_copy(
-            src_ref=res.at[0, own_rows(member(d)), columns(j)],
+            src_ref=res_hbm.at[0, own_rows(member(d)), columns(j)],
             dst_ref=raw.at[j, d - 1],
             send_sem=raw_send.at[j, d - 1],
             recv_sem=raw_recv.at[j, d - 1],
@@ -97,6 +107,11 @@
             device_id={"chan": lax.rem(k + depth - 1, depth)}, device_id_type=MESH,
         )
 
+    def out_copy(j):
+        return pltpu.make_async_copy(
+            result.at[j], new_out.at[0, :, columns(j)], out_sem.at[j]
+        )
+
     def send_raw(j, carry):
         for d in range(1, tiles):
             raw_copy(j, d).start()
@@ -112,6 +127,7 @@
         y = x * x
         return sums[0] + x, sums[1] + y, sums[2] + x * y, sums[3] + y * y
 
+    loads[0].wait()
     zero = jnp.float32(0.0)
     s1, s2, s3, s4 = lax.fori_loop(0, total, add_powers, (zero, zero, zero, zero))
     m = ((jnp.float32(total), s1, s2), (s1, s2, s3), (s2, s3, s4))
@@ -129,27 +145,22 @@
         weight_s[2 * d] = x
         weight_s[2 * d + 1] = x * x
 
-    profile[...] = jnp.zeros_like(profile)
-    profile[:, 0 : psf.shape[2]] = psf[0]
-    wide = profile.shape[1]
-    band = pltpu.roll(
-        jnp.broadcast_to(profile[1:2, :], (CHUNK, wide)), 0, 1, stride=1, stride_axis=0
-    )
-    row_high[...], row_low[...] = split_halves(band)
-    half = (psf.shape[2] - 1) // 2
-    band = pltpu.roll(
-        jnp.broadcast_to(profile[0:1, :], (height, wide)), wide - half, 1, stride=1, stride_axis=0
-    )[:, :height]
-    col_high[...], col_low[...] = split_halves(band)
     model[0] = jnp.zeros(model.shape[1:], jnp.float32)
     model[chunks + 1] = jnp.zeros(model.shape[1:], jnp.float32)
 
-    lag_left = HOP * k
-    lag_right = HOP * (depth - 1 - k)
+    loads[2].wait()
+    def lag_of(hops):
+        return HOP * hops
+
+    lag_left = lag_of(k)
+    lag_right = lag_of(depth - 1 - k)
     lag = jnp.maximum(lag_left, lag_right)
 
     def inside(j):
         return jnp.logical_and(j >= 0, j < chunks)
+
+    half = (psf.shape[2] - 1) // 2
+    wide = profile.shape[1]
 
     def step(s, carry):
         @pl.when(s < chunks)
@@ -229,6 +240,20 @@
                 model_copy(jt, d).start()
             model[jt + 1, own_rows(a)] = u[0] + weight_s[0] * u[1] + weight_s[1] * u[2]
 
+        @pl.when(s == 1)
+        def _():
+            loads[1].wait()
+            profile[...] = jnp.zeros_like(profile)
+            profile[:, 0 : psf.shape[2]] = psf[0]
+            band = pltpu.roll(
+                jnp.broadcast_to(profile[1:2, :], (CHUNK, wide)), 0, 1, stride=1, stride_axis=0
+            )
+            row_high[...], row_low[...] = split_halves(band)
+            band = pltpu.roll(
+                jnp.broadcast_to(profile[0:1, :], (height, wide)), wide - half, 1, stride=1, stride_axis=0
+            )[:, :height]
+            col_high[...], col_low[...] = split_halves(band)
+
         jb = jt - BACK
 
         @pl.when(jnp.logical_and(jb + 1 >= 0, jb + 1 < chunks))
@@ -243,17 +268,25 @@
             )
             rowwise = dot_split(split_halves(field), (row_high[...], row_low[...]), ((1,), (1,)))
             blurred = dot_split((col_high[...], col_low[...]), split_halves(rowwise), ((1,), (0,)))
-            new_out[0, :, columns(jb)] = res[0, :, columns(jb)] - blurred
+            result[jb] = res[0, :, columns(jb)] - blurred
+            out_copy(jb).start()
 
         return carry
 
-    lax.fori_loop(0, chunks + HOP * (depth - 1) + BACK, step, 0)
+    lax.fori_loop(0, chunks + lag_of(depth - 1) + BACK, step, 0)
 
     per = taylor_out.shape[2] // CHUNK
-    for i in range(per):
-        taylor_out[:, :, i * CHUNK : (i + 1) * CHUNK] = steps[k * per + i]
+    saves = [
+        pltpu.make_async_copy(
+            steps.at[k * per + i], taylor_out.at[:, :, pl.ds(i * CHUNK, CHUNK)], step_sem.at[i]
+        )
+        for i in range(per)
+    ]
+    for save in saves:
+        save.start()
 
     def drain(j, carry):
+        out_copy(j).wait()
         for d in range(1, tiles):
             raw_copy(j, d).wait_send()
             model_copy(j, d).wait_send()
@@ -269,6 +302,8 @@
         return carry
 
     lax.fori_loop(0, chunks, drain, 0)
+    for save in saves:
+        save.wait()
 
 
 def solution(mesh):
@@ -281,7 +316,7 @@
         half = (psf_profile.shape[2] - 1) // 2
         f32, bf16 = jnp.float32, jnp.bfloat16
         chain = pltpu.VMEM((chunks, 3, rows, CHUNK), f32)
-        vmem = pl.BlockSpec(memory_space=pltpu.VMEM)
+        anywhere = pl.BlockSpec(memory_space=pltpu.HBM)
         dma = pltpu.SemaphoreType.DMA
         return pl.pallas_call(
             functools.partial(kernel, tiles, depth, chunks),
@@ -289,9 +324,13 @@
                 jax.ShapeDtypeStruct((3, rows, block), f32),
                 jax.ShapeDtypeStruct(residual.shape, f32),
             ),
-            in_specs=[vmem, pl.BlockSpec(memory_space=pltpu.SMEM), vmem],
-            out_specs=(vmem, vmem),
+            in_specs=[anywhere] * 3,
+            out_specs=(anywhere, anywhere),
             scratch_shapes=[
+                pltpu.VMEM(residual.shape, f32),
+                pltpu.SMEM(freq_index.shape, jnp.int32),
+                pltpu.VMEM(psf_profile.shape, f32),
+                pltpu.VMEM((chunks, height, CHUNK), f32),
                 pltpu.VMEM((chunks, tiles - 1, rows, CHUNK), f32),
                 chain, chain, chain, chain, chain, chain,
                 pltpu.VMEM((chunks, tiles - 1, rows, CHUNK), f32),
@@ -305,6 +344,7 @@
                 dma((chunks, tiles - 1)), dma((chunks, tiles - 1)),
                 dma((chunks, tiles - 1)), dma((chunks, tiles - 1)),
                 dma((chunks,)), dma((chunks,)), dma((chunks,)), dma((chunks,)),
+                dma((3,)), dma((chunks,)), dma((block // CHUNK,)),
             ],
             compiler_params=pltpu.CompilerParams(
                 collective_id=0, has_side_effects=True, vmem_limit_bytes=40 * 1024 * 1024

time: 45.9 us -> 44.7 us (0.974)
  Pallas kernels: 40.9 us -> 39.7 us
    pallas_call x1, Pallas kernels: 40.9 us -> 39.7 us  [shards(): pl.pallas_call(functools.partial(kernel, tiles, depth, chunks), out_shape...]
where the time goes in v3:
time: 44.7 us; the launch traced here: 44.5 us
  Pallas kernels  39.7 us (89%)
  local copies, waits for them, and re-layouts  4.21 us (9%)
  between operations  0.65 us (1%)
    pallas_call x1, Pallas kernels, shards(): pl.pallas_call(functools.partial(kernel, tiles, depth, chunks), out_shape...  39.7 us
    unnamed x8, local copies, waits for them, and re-layouts  4.21 us

profile of v3, /device:TPU:0, one launch (start us, length us, event | category | flops | bytes accessed | tf_op | source)
XLA Modules:
  0.0 44.5 jit_solution(12665928490943355749)
XLA Ops:
  0.6 0.0 copy-start
  0.6 1.2 %copy-done = f32[1,128,2048]{2,1,0:T(8,128)S(1)} copy-done((f32[1,128,2048]{2,1,0:T(8,128)S(1)}, f32[1,128,2048]{2,1,0:T(8,128)}, u32[]{:S(2)}) %copy-start) | copy-done | bytes 1048600
  1.9 0.0 copy-start.1
  1.9 0.7 %copy-done.1 = f32[1,2,257]{2,1,0:T(2,128)S(1)} copy-done((f32[1,2,257]{2,1,0:T(2,128)S(1)}, f32[1,2,257]{2,1,0:T(2,128)}, u32[]{:S(2)}) %copy-start.1) | copy-done | bytes 2080
  2.5 0.0 copy-start.2
  2.5 0.7 %copy-done.2 = s32[16]{0:T(128)S(1)} copy-done((s32[16]{0:T(128)S(1)}, s32[16]{0:T(128)}, u32[]{:S(2)}) %copy-start.2) | copy-done | bytes 88
  3.2 39.7 %shard_map.50 = (f32[3,32,512]{2,1,0:T(8,128)S(1)}, f32[1,128,2048]{2,1,0:T(8,128)S(1)}) custom-call(f32[1,128,2048]{2,1,0:T(8,128)S(1)} %copy-done, s32[16]{0:T(128)S(1)} %copy-done.2, f32[1,2,257]{2,1,0:T(2,128)S(1)} %copy-done.1), custom_call_target="tpu_custom_call" | custom-call | tf_op jit(solution)/shard_map/pallas_call | solution.py:321
  42.9 0.7 %copy.7 = f32[3,32,512]{2,1,0:T(8,128)} copy(f32[3,32,512]{2,1,0:T(8,128)S(1)} %get-tuple-element.4) | data formatting | bytes 393216
  43.6 1.0 %copy.8 = f32[1,128,2048]{2,1,0:T(8,128)} copy(f32[1,128,2048]{2,1,0:T(8,128)S(1)} %get-tuple-element.5) | data formatting | bytes 2097152
Async XLA Ops:
  0.6 1.2 %copy-start = (f32[1,128,2048]{2,1,0:T(8,128)S(1)}, f32[1,128,2048]{2,1,0:T(8,128)}, u32[]{:S(2)}) copy-start(f32[1,128,2048]{2,1,0:T(8,128)} %res_hbm.1) | copy-start | bytes 3145732
  1.9 0.7 %copy-start.1 = (f32[1,2,257]{2,1,0:T(2,128)S(1)}, f32[1,2,257]{2,1,0:T(2,128)}, u32[]{:S(2)}) copy-start(f32[1,2,257]{2,1,0:T(2,128)} %psf_hbm.1) | copy-start | bytes 6172
  2.5 0.7 %copy-start.2 = (s32[16]{0:T(128)S(1)}, s32[16]{0:T(128)}, u32[]{:S(2)}) copy-start(s32[16]{0:T(128)} %freq_hbm.1) | copy-start | bytes 196

commit v4 on v3

--- a/solution.py
+++ b/solution.py
@@ -12,6 +12,7 @@
 HOP = 4
 BACK = 6
 CHUNK = 128
+BLOCK = 2 * CHUNK
 
 
 def split_halves(x):
@@ -107,9 +108,12 @@
             device_id={"chan": lax.rem(k + depth - 1, depth)}, device_id_type=MESH,
         )
 
+    def pair_columns(j):
+        return pl.ds(pl.multiple_of(j * BLOCK, BLOCK), BLOCK)
+
     def out_copy(j):
         return pltpu.make_async_copy(
-            result.at[j], new_out.at[0, :, columns(j)], out_sem.at[j]
+            result.at[j], new_out.at[0, :, pair_columns(j)], out_sem.at[j]
         )
 
     def send_raw(j, carry):
@@ -246,7 +250,7 @@
             profile[...] = jnp.zeros_like(profile)
             profile[:, 0 : psf.shape[2]] = psf[0]
             band = pltpu.roll(
-                jnp.broadcast_to(profile[1:2, :], (CHUNK, wide)), 0, 1, stride=1, stride_axis=0
+                jnp.broadcast_to(profile[1:2, :], (BLOCK, wide)), 0, 1, stride=1, stride_axis=0
             )
             row_high[...], row_low[...] = split_halves(band)
             band = pltpu.roll(
@@ -261,15 +265,17 @@
             for d in range(1, tiles):
                 model_copy(jb + 1, d).wait_recv()
 
-        @pl.when(inside(jb))
+        @pl.when(jnp.logical_and(inside(jb), lax.rem(jb + 2 * chunks, 2) == 1))
         def _():
             field = jnp.concatenate(
-                [model[jb, :, CHUNK - half :], model[jb + 1], model[jb + 2, :, :half]], axis=1
+                [model[jb - 1, :, CHUNK - half :], model[jb], model[jb + 1], model[jb + 2, :, :half]],
+                axis=1,
             )
             rowwise = dot_split(split_halves(field), (row_high[...], row_low[...]), ((1,), (1,)))
             blurred = dot_split((col_high[...], col_low[...]), split_halves(rowwise), ((1,), (0,)))
-            result[jb] = res[0, :, columns(jb)] - blurred
-            out_copy(jb).start()
+            pair = jb // 2
+            result[pair] = res[0, :, pair_columns(pair)] - blurred
+            out_copy(pair).start()
 
         return carry
 
@@ -286,7 +292,6 @@
         save.start()
 
     def drain(j, carry):
-        out_copy(j).wait()
         for d in range(1, tiles):
             raw_copy(j, d).wait_send()
             model_copy(j, d).wait_send()
@@ -302,6 +307,8 @@
         return carry
 
     lax.fori_loop(0, chunks, drain, 0)
+    for i in range(chunks // 2):
+        out_copy(i).wait()
     for save in saves:
         save.wait()
 
@@ -330,21 +337,21 @@
                 pltpu.VMEM(residual.shape, f32),
                 pltpu.SMEM(freq_index.shape, jnp.int32),
                 pltpu.VMEM(psf_profile.shape, f32),
-                pltpu.VMEM((chunks, height, CHUNK), f32),
+                pltpu.VMEM((chunks // 2, height, BLOCK), f32),
                 pltpu.VMEM((chunks, tiles - 1, rows, CHUNK), f32),
                 chain, chain, chain, chain, chain, chain,
                 pltpu.VMEM((chunks, tiles - 1, rows, CHUNK), f32),
                 pltpu.VMEM((chunks + 2, height, CHUNK), f32),
-                pltpu.VMEM((2, CHUNK + 2 * half), f32),
-                pltpu.VMEM((CHUNK, CHUNK + 2 * half), bf16),
-                pltpu.VMEM((CHUNK, CHUNK + 2 * half), bf16),
+                pltpu.VMEM((2, BLOCK + 2 * half), f32),
+                pltpu.VMEM((BLOCK, BLOCK + 2 * half), bf16),
+                pltpu.VMEM((BLOCK, BLOCK + 2 * half), bf16),
                 pltpu.VMEM((height, height), bf16),
                 pltpu.VMEM((height, height), bf16),
                 pltpu.SMEM((2 * tiles + 9,), f32),
                 dma((chunks, tiles - 1)), dma((chunks, tiles - 1)),
                 dma((chunks, tiles - 1)), dma((chunks, tiles - 1)),
                 dma((chunks,)), dma((chunks,)), dma((chunks,)), dma((chunks,)),
-                dma((3,)), dma((chunks,)), dma((block // CHUNK,)),
+                dma((3,)), dma((chunks // 2,)), dma((block // CHUNK,)),
             ],
             compiler_params=pltpu.CompilerParams(
                 collective_id=0, has_side_effects=True, vmem_limit_bytes=40 * 1024 * 1024

time: 44.7 us -> 44.5 us (level)
  no operation moved by 1% of the time
where the time goes in v4:
time: 44.5 us; the launch traced here: 44.4 us
  Pallas kernels  39.5 us (89%)
  local copies, waits for them, and re-layouts  4.21 us (9%)
  between operations  0.65 us (1%)
    pallas_call x1, Pallas kernels, shards(): pl.pallas_call(functools.partial(kernel, tiles, depth, chunks), out_shape...  39.5 us
    unnamed x8, local copies, waits for them, and re-layouts  4.21 us

profile of v4, /device:TPU:0, one launch (start us, length us, event | category | flops | bytes accessed | tf_op | source)
XLA Modules:
  0.0 44.4 jit_solution(2187846798381264657)
XLA Ops:
  0.6 0.0 copy-start
  0.6 1.2 %copy-done = f32[1,128,2048]{2,1,0:T(8,128)S(1)} copy-done((f32[1,128,2048]{2,1,0:T(8,128)S(1)}, f32[1,128,2048]{2,1,0:T(8,128)}, u32[]{:S(2)}) %copy-start) | copy-done | bytes 1048600
  1.9 0.0 copy-start.1
  1.9 0.7 %copy-done.1 = f32[1,2,257]{2,1,0:T(2,128)S(1)} copy-done((f32[1,2,257]{2,1,0:T(2,128)S(1)}, f32[1,2,257]{2,1,0:T(2,128)}, u32[]{:S(2)}) %copy-start.1) | copy-done | bytes 2080
  2.5 0.0 copy-start.2
  2.5 0.7 %copy-done.2 = s32[16]{0:T(128)S(1)} copy-done((s32[16]{0:T(128)S(1)}, s32[16]{0:T(128)}, u32[]{:S(2)}) %copy-start.2) | copy-done | bytes 88
  3.2 39.5 %shard_map.50 = (f32[3,32,512]{2,1,0:T(8,128)S(1)}, f32[1,128,2048]{2,1,0:T(8,128)S(1)}) custom-call(f32[1,128,2048]{2,1,0:T(8,128)S(1)} %copy-done, s32[16]{0:T(128)S(1)} %copy-done.2, f32[1,2,257]{2,1,0:T(2,128)S(1)} %copy-done.1), custom_call_target="tpu_custom_call" | custom-call | tf_op jit(solution)/shard_map/pallas_call | solution.py:328
  42.7 0.7 %copy.7 = f32[3,32,512]{2,1,0:T(8,128)} copy(f32[3,32,512]{2,1,0:T(8,128)S(1)} %get-tuple-element.4) | data formatting | bytes 393216
  43.4 1.0 %copy.8 = f32[1,128,2048]{2,1,0:T(8,128)} copy(f32[1,128,2048]{2,1,0:T(8,128)S(1)} %get-tuple-element.5) | data formatting | bytes 2097152
Async XLA Ops:
  0.6 1.2 %copy-start = (f32[1,128,2048]{2,1,0:T(8,128)S(1)}, f32[1,128,2048]{2,1,0:T(8,128)}, u32[]{:S(2)}) copy-start(f32[1,128,2048]{2,1,0:T(8,128)} %res_hbm.1) | copy-start | bytes 3145732
  1.9 0.7 %copy-start.1 = (f32[1,2,257]{2,1,0:T(2,128)S(1)}, f32[1,2,257]{2,1,0:T(2,128)}, u32[]{:S(2)}) copy-start(f32[1,2,257]{2,1,0:T(2,128)} %psf_hbm.1) | copy-start | bytes 6172
  2.5 0.7 %copy-start.2 = (s32[16]{0:T(128)S(1)}, s32[16]{0:T(128)}, u32[]{:S(2)}) copy-start(s32[16]{0:T(128)} %freq_hbm.1) | copy-start | bytes 196

commit v5 on v4

--- a/solution.py
+++ b/solution.py
@@ -117,7 +117,7 @@
         )
 
     def send_raw(j, carry):
-        for d in range(1, tiles):
+        for d in (*range(2, tiles), 1):
             raw_copy(j, d).start()
         return carry
 
@@ -239,7 +239,7 @@
             ]
             for t in range(3):
                 steps[jt, t] = u[t]
-            for d in range(1, tiles):
+            for d in (*range(2, tiles), 1):
                 outgoing[jt, d - 1] = u[0] + weight_s[2 * d] * u[1] + weight_s[2 * d + 1] * u[2]
                 model_copy(jt, d).start()
             model[jt + 1, own_rows(a)] = u[0] + weight_s[0] * u[1] + weight_s[1] * u[2]

time: 44.5 us -> 44.2 us (level)
  no operation moved by 1% of the time
where the time goes in v5:
time: 44.2 us; the launch traced here: 44 us
  Pallas kernels  39.2 us (89%)
  local copies, waits for them, and re-layouts  4.21 us (10%)
  between operations  0.65 us (1%)
    pallas_call x1, Pallas kernels, shards(): pl.pallas_call(functools.partial(kernel, tiles, depth, chunks), out_shape...  39.2 us
    unnamed x8, local copies, waits for them, and re-layouts  4.21 us

profile of v5, /device:TPU:0, one launch (start us, length us, event | category | flops | bytes accessed | tf_op | source)
XLA Modules:
  0.0 44.0 jit_solution(8170862746431591820)
XLA Ops:
  0.6 0.0 copy-start
  0.6 1.2 %copy-done = f32[1,128,2048]{2,1,0:T(8,128)S(1)} copy-done((f32[1,128,2048]{2,1,0:T(8,128)S(1)}, f32[1,128,2048]{2,1,0:T(8,128)}, u32[]{:S(2)}) %copy-start) | copy-done | bytes 1048600
  1.9 0.0 copy-start.1
  1.9 0.7 %copy-done.1 = f32[1,2,257]{2,1,0:T(2,128)S(1)} copy-done((f32[1,2,257]{2,1,0:T(2,128)S(1)}, f32[1,2,257]{2,1,0:T(2,128)}, u32[]{:S(2)}) %copy-start.1) | copy-done | bytes 2080
  2.5 0.0 copy-start.2
  2.5 0.7 %copy-done.2 = s32[16]{0:T(128)S(1)} copy-done((s32[16]{0:T(128)S(1)}, s32[16]{0:T(128)}, u32[]{:S(2)}) %copy-start.2) | copy-done | bytes 88
  3.2 39.2 %shard_map.50 = (f32[3,32,512]{2,1,0:T(8,128)S(1)}, f32[1,128,2048]{2,1,0:T(8,128)S(1)}) custom-call(f32[1,128,2048]{2,1,0:T(8,128)S(1)} %copy-done, s32[16]{0:T(128)S(1)} %copy-done.2, f32[1,2,257]{2,1,0:T(2,128)S(1)} %copy-done.1), custom_call_target="tpu_custom_call" | custom-call | tf_op jit(solution)/shard_map/pallas_call | solution.py:328
  42.4 0.7 %copy.7 = f32[3,32,512]{2,1,0:T(8,128)} copy(f32[3,32,512]{2,1,0:T(8,128)S(1)} %get-tuple-element.4) | data formatting | bytes 393216
  43.1 1.0 %copy.8 = f32[1,128,2048]{2,1,0:T(8,128)} copy(f32[1,128,2048]{2,1,0:T(8,128)S(1)} %get-tuple-element.5) | data formatting | bytes 2097152
Async XLA Ops:
  0.6 1.2 %copy-start = (f32[1,128,2048]{2,1,0:T(8,128)S(1)}, f32[1,128,2048]{2,1,0:T(8,128)}, u32[]{:S(2)}) copy-start(f32[1,128,2048]{2,1,0:T(8,128)} %res_hbm.1) | copy-start | bytes 3145732
  1.9 0.7 %copy-start.1 = (f32[1,2,257]{2,1,0:T(2,128)S(1)}, f32[1,2,257]{2,1,0:T(2,128)}, u32[]{:S(2)}) copy-start(f32[1,2,257]{2,1,0:T(2,128)} %psf_hbm.1) | copy-start | bytes 6172
  2.5 0.7 %copy-start.2 = (s32[16]{0:T(128)S(1)}, s32[16]{0:T(128)}, u32[]{:S(2)}) copy-start(s32[16]{0:T(128)} %freq_hbm.1) | copy-start | bytes 196
